TPU v7x, 256 devices: a whole 4x4x8 slice. The times are simulated.
256 devices in a mesh: seq: 32 (over z, x), head: 8 (over y, core).
Axes of the slice: x: 4, y: 4, z: 8, core: 2. Of those that a mesh axis runs over, the one named last changes fastest.
Arguments:
- states: bfloat16 [16384, 4096], P('seq'), may hold values from -6 to 256
- w_query: bfloat16 [4096, 4096], P('seq', 'head'), may hold values from -1 to 1
- w_output: bfloat16 [4096, 4096], P('head', 'seq'), may hold values from -0.09375 to 0.09375
- kv_store: bfloat16 [256, 2, 128, 4096], P('seq', None, None, 'head'), may hold values from -140 to 140
- neighbour_ids: int32 [256, 2], P('seq'), may hold values from 0 to 255, as said below
- block_row: int32 [256], replicated, may hold values from 0 to 255, as said below
Outputs:
- mixed: bfloat16 [16384, 4096], P('seq', 'head')
Inputs may be any that keep to these rules, and one draw needn't show every extreme that they name: `block_row`: A permutation of 0 to 255; row r of kv_store lies on index r // 8 of seq. `neighbour_ids`: of the 16 neighbours of one index of seq, at most 2 lie in rows of kv_store held by any one index of seq; one such holder has exactly 2 of every index's neighbours.
All inputs are finite; a program needn't handle non-finite values.
Results may differ from a plain program's by a relative error of at most 0.019.
Values may be sent and summed in bfloat16 or wider, within the bound.
A program may use at most 128 MiB of HBM per device.

v0:
```python
import jax
import jax.numpy as jnp
from jax import lax
from jax.sharding import PartitionSpec as P

HD = 128
STRETCH = 64
NB_TOK = 128


def shifted(shard, axis, by):
    length = lax.axis_size(axis)
    pairs = [(i, i + by) for i in range(length) if 0 <= i + by < length]
    return lax.ppermute(shard, axis, pairs)


def partial_attend(query_block, kv_blocks):
    count, rows, width = query_block.shape
    nheads = width // HD
    qhead = query_block.reshape(count, rows, nheads, HD)
    keys = kv_blocks[:, 0].reshape(count, NB_TOK, nheads, HD)
    values = kv_blocks[:, 1].reshape(count, NB_TOK, nheads, HD)
    scores = jnp.einsum("nqhd,nkhd->nhqk", qhead, keys, preferred_element_type=jnp.float32) * (
        1.0 / HD**0.5
    )
    maxima = jnp.max(scores, axis=-1)
    weights = jnp.exp(scores - maxima[..., None]).astype(jnp.bfloat16)
    totals = jnp.sum(weights, axis=-1, dtype=jnp.float32)
    outputs = jnp.einsum("nhqk,nkhd->nqhd", weights, values, preferred_element_type=jnp.float32)
    return (outputs.reshape(count, rows, width), maxima, totals)


def combine_pair(outputs, maxima, totals):
    spans, neigh, rows, width = outputs.shape
    nheads = width // HD
    top = jnp.max(maxima, axis=1)
    factor = jnp.exp(maxima - top[:, None])
    denom = jnp.sum(factor * totals, axis=1)
    spread = jnp.transpose(factor, (0, 1, 3, 2))[..., None]
    numer = jnp.sum(outputs.reshape(spans, neigh, rows, nheads, HD) * spread, axis=1)
    result = numer / jnp.transpose(denom, (0, 2, 1))[..., None]
    return result.reshape(spans, rows, width).astype(jnp.bfloat16)


def local(states, w_query, w_output, kv_store, neighbour_ids, block_row):
    tok_rows = states.shape[0]
    width = w_query.shape[1]
    span_count, neigh = neighbour_ids.shape
    requests = span_count * neigh
    nseq = lax.axis_size("seq")
    slot_count = max(2, (2 * requests + nseq - 1) // nseq)
    blk_dev = kv_store.shape[0]
    position = lax.axis_index("seq")
    starts_here = position == 0
    next_starts = position == nseq - 1
    queries = jnp.dot(
        states,
        lax.all_gather(w_query, "seq", axis=0, tiled=True),
        preferred_element_type=jnp.float32,
    ).astype(jnp.bfloat16)
    leading = shifted(queries[: STRETCH - 1], "seq", -1)
    leading = jnp.where(next_starts, jnp.zeros_like(leading), leading)
    groups = jnp.concatenate([queries[STRETCH - 1 :], leading], axis=0).reshape(
        span_count, STRETCH, width
    )
    query_req = jnp.repeat(groups, neigh, axis=0)
    flat_ids = neighbour_ids.reshape(requests)
    table_cols = jnp.arange(block_row.shape[0], dtype=jnp.int32)
    store_row = jnp.sum(
        jnp.where(flat_ids[:, None] == table_cols[None, :], block_row[None, :], 0), axis=1
    )
    holders = store_row // blk_dev
    block_slot = store_row % blk_dev
    counter = jnp.arange(requests, dtype=jnp.int32)
    earlier = (holders[:, None] == holders[None, :]) & (counter[:, None] > counter[None, :])
    slot_rank = jnp.sum(earlier.astype(jnp.int32), axis=1)
    buffer_index = holders * slot_count + slot_rank
    slot_table = (
        jnp.zeros((nseq * slot_count,), jnp.int32)
        .at[buffer_index]
        .set(block_slot)
        .reshape(nseq, slot_count)
    )
    asked = lax.all_to_all(slot_table, "seq", split_axis=0, concat_axis=0, tiled=True)
    served = kv_store[asked.reshape(nseq * slot_count)].reshape(nseq, slot_count, 2, NB_TOK, width)
    fetched = lax.all_to_all(served, "seq", split_axis=0, concat_axis=0, tiled=True)
    kv_req = fetched.reshape(nseq * slot_count, 2, NB_TOK, width)[buffer_index]
    outputs, maxima, totals = partial_attend(query_req, kv_req)
    nheads = maxima.shape[1]
    context_groups = combine_pair(
        outputs.reshape(span_count, neigh, STRETCH, width),
        maxima.reshape(span_count, neigh, nheads, STRETCH),
        totals.reshape(span_count, neigh, nheads, STRETCH),
    )
    extended = context_groups.reshape(tok_rows, width)
    trailing = shifted(extended[tok_rows - STRETCH + 1 :], "seq", 1)
    trailing = jnp.where(starts_here, jnp.zeros_like(trailing), trailing)
    context = jnp.concatenate([trailing, extended[: tok_rows - STRETCH + 1]], axis=0)
    terms = jnp.dot(
        context,
        lax.all_gather(w_output, "seq", axis=1, tiled=True),
        preferred_element_type=jnp.float32,
    )
    return lax.psum_scatter(terms.astype(jnp.bfloat16), "head", scatter_dimension=1, tiled=True)


def solution(mesh):
    in_specs = (
        P("seq", None),
        P("seq", "head"),
        P("head", "seq"),
        P("seq", None, None, "head"),
        P("seq", None),
        P(),
    )
    out_specs = P("seq", "head")
    return jax.shard_map(local, mesh=mesh, in_specs=in_specs, out_specs=out_specs, check_vma=False)
```

profile of v0, /device:TPU:2, one launch (start us, length us, event | category | flops | bytes accessed | tf_op | source)
XLA Modules:
  0.0 576.8 jit_solution(16205739280007865709)
XLA Ops:
  6.5 0.9 copy.26
  7.5 0.9 select_reduce_fusion
  8.4 0.2 convert_reduce_fusion.1
  8.6 0.6 scatter_custom_fusion
  9.3 19.9 %all_to_all.14 = s32[32,1,2]{2,1,0:T(1,128)S(1)} all-to-all(s32[32,1,2]{2,1,0:T(1,128)S(1)} %bitcast.62), channel_id=1, replica_groups=mesh['seq'=32,'head'=8] {'seq'}, dimensions={0} | all-to-all | bytes 512 | tf_op jit(solution)/shard_map/all_to_all | solution.py:84
  29.3 0.5 broadcast.198
  29.8 0.7 reduce.3
  30.6 7.3 %gather_fusion = bf16[64,2,128,512]{3,2,1,0:T(8,128)(2,1)} fusion(bf16[8,2,128,512]{3,2,1,0:T(8,128)(2,1)S(1)} %copy-done, s32[1024]{0:T(1024)S(1)} %pad_clamp_fusion.1), kind=kCustom, calls=%fused_computation | custom fusion | bytes 33554688 | tf_op jit(solution)/shard_map/gather | solution.py:85
  37.9 6.2 %all-to-all-start.1 = ((bf16[32,2,2,128,512]{4,3,2,1,0:T(8,128)(2,1)}), bf16[32,2,2,128,512]{4,3,2,1,0:T(8,128)(2,1)}, u32[]{:S(2)}, u32[]{:S(2)}) async-start(bf16[32,2,2,128,512]{4,3,2,1,0:T(8,128)(2,1)} %bitcast.54), calls=%async_computation.1 | async-start | bytes 33554432 | tf_op jit(solution)/shard_map/all_to_all | solution.py:86
  44.2 0.7 all-gather.3.cloned.1.call-update
  44.9 0.7 all-gather.5.cloned.1.call-update
  45.7 184.7 %all-gather.3.cloned.1.call-done = bf16[4096,512]{1,0:T(8,128)(2,1)} async-done(((bf16[128,512]{1,0:T(8,128)(2,1)}), bf16[4096,512]{1,0:T(8,128)(2,1)}) %all-gather.3.cloned.1.call-update) | async-done | bytes 4194320 | tf_op jit(solution)/shard_map/all_gather | solution.py:58
  230.4 5.8 %convolution_convert_fusion.1 = bf16[512,512]{1,0:T(8,128)(2,1)S(1)} fusion(bf16[512,4096]{1,0:T(8,128)(2,1)} %param.6, bf16[4096,512]{1,0:T(8,128)(2,1)} %all-gather.3.cloned.1.call-done), kind=kOutput, calls=%fused_computation.8 | convolution fusion | flops 2147745792 | bytes 8912896 | tf_op jit(solution)/shard_map/dot_general | solution.py:56
  236.2 1.9 collective-permute-start
  238.1 0.1 slice.29
  238.3 18.8 %collective-permute-done = bf16[63,512]{1,0:T(8,128)(2,1)S(1)} collective-permute-done((bf16[63,512]{1,0:T(8,128)(2,1)S(1)}, bf16[63,512]{1,0:T(8,128)(2,1)S(1)}, u32[]{:S(2)}, u32[]{:S(2)}) %collective-permute-start) | collective-permute-done | bytes 64544 | tf_op jit(solution)/shard_map/ppermute | solution.py:14
  257.2 0.3 reshape_reshape.3
  257.5 201.7 %all-to-all-done.1 = bf16[32,2,2,128,512]{4,3,2,1,0:T(8,128)(2,1)} async-done(((bf16[32,2,2,128,512]{4,3,2,1,0:T(8,128)(2,1)}), bf16[32,2,2,128,512]{4,3,2,1,0:T(8,128)(2,1)}, u32[]{:S(2)}, u32[]{:S(2)}) %all-to-all-start.1) | async-done | bytes 16777248 | tf_op jit(solution)/shard_map/all_to_all | solution.py:86
  459.2 8.6 %gather_fusion.1 = bf16[16,2,128,512]{3,2,1,0:T(8,128)(2,1)} fusion(bf16[64,2,128,512]{3,2,1,0:T(8,128)(2,1)} %bitcast.6, s32[1024]{0:T(1024)S(1)} %pad_clamp_fusion), kind=kCustom, calls=%fused_computation.1 | custom fusion | bytes 8388672 | tf_op jit(solution)/shard_map/gather | solution.py:87
  467.8 4.0 fusion.15
  471.8 3.9 copy.29
  475.7 2.4 copy.28
  478.2 2.4 multiply_reduce_fusion.1
  480.6 1.3 convert_reduce_fusion
  481.9 0.2 copy-done.2
  482.1 1.8 multiply_reduce_fusion
  483.9 0.3 divide_convert_fusion
  484.3 0.4 copy.33
  484.8 1.9 collective-permute-start.1
  486.8 20.4 %collective-permute-done.1 = bf16[63,512]{1,0:T(8,128)(2,1)S(1)} collective-permute-done((bf16[63,512]{1,0:T(8,128)(2,1)S(1)}, bf16[63,512]{1,0:T(8,128)(2,1)S(1)}, u32[]{:S(2)}, u32[]{:S(2)}) %collective-permute-start.1) | collective-permute-done | bytes 64544 | tf_op jit(solution)/shard_map/ppermute | solution.py:14
  507.2 6.5 %convolution_convert_fusion = bf16[512,4096]{1,0:T(8,128)(2,1)} fusion(bf16[512,4096]{1,0:T(8,128)(2,1)} %all-gather.5.cloned.1.call-done, bf16[449,512]{1,0:T(8,128)(2,1)S(1)} %slice.33, bf16[63,512]{1,0:T(8,128)(2,1)S(1)} %broadcast_select_fusion.1), kind=kOutput, calls=%fused_computation.3 | convolution fusion | flops 2150629376 | bytes 8912896 | tf_op jit(solution)/shard_map/dot_general | solution.py:99
  513.7 56.6 %reduce-scatter.2.cloned.1.call-done = bf16[512,512]{1,0:T(8,128)(2,1)} async-done(((bf16[512,4096]{1,0:T(8,128)(2,1)}), bf16[512,512]{1,0:T(8,128)(2,1)}) %reduce-scatter.2.cloned.1.call-update) | async-done | bytes 524304 | tf_op jit(solution)/shard_map/reduce_scatter | solution.py:104
  (28 shorter events, 0.8 us)
Async XLA Ops:
  6.5 24.1 %copy-start = (bf16[8,2,128,512]{3,2,1,0:T(8,128)(2,1)S(1)}, bf16[8,2,128,512]{3,2,1,0:T(8,128)(2,1)}, u32[]{:S(2)}) copy-start(bf16[8,2,128,512]{3,2,1,0:T(8,128)(2,1)} %param.9) | copy-start | bytes 6291460
  37.9 421.3 %all-to-all-start.1 = ((bf16[32,2,2,128,512]{4,3,2,1,0:T(8,128)(2,1)}), bf16[32,2,2,128,512]{4,3,2,1,0:T(8,128)(2,1)}, u32[]{:S(2)}, u32[]{:S(2)}) async-start(bf16[32,2,2,128,512]{4,3,2,1,0:T(8,128)(2,1)} %bitcast.54), calls=%async_computation.1 | async-start | bytes 33554432 | tf_op jit(solution)/shard_map/all_to_all | solution.py:86
  44.1 186.2 %all-gather.3.cloned.1.call-start = ((), (), s32[]{:S(2)}) async-start(), calls=%async_computation.3 | async-start | bytes 4325376 | tf_op jit(solution)/shard_map/all_gather | solution.py:58
  44.9 462.4 %all-gather.5.cloned.1.call-start = ((), (), s32[]{:S(2)}) async-start(), calls=%async_computation.4 | async-start | bytes 4325376 | tf_op jit(solution)/shard_map/all_gather | solution.py:101
  45.6 524.7 %reduce-scatter.2.cloned.1.call-start = ((), (), s32[]{:S(2)}) async-start(), calls=%async_computation.5 | async-start | bytes 4718592 | tf_op jit(solution)/shard_map/reduce_scatter | solution.py:104
  236.2 20.9 %collective-permute-start = (bf16[63,512]{1,0:T(8,128)(2,1)S(1)}, bf16[63,512]{1,0:T(8,128)(2,1)S(1)}, u32[]{:S(2)}, u32[]{:S(2)}) collective-permute-start(bf16[63,512]{1,0:T(8,128)(2,1)S(1)} %slice.30), channel_id=1, source_target_pairs={{8,0},{16,8},{24,16},{32,24},{40,32},{48,40},{56,48},{64,56},{72,6... | collective-permute-start | bytes 193544 | tf_op jit(solution)/shard_map/ppermute | solution.py:14
  480.5 1.6 copy-start.2
  484.8 22.4 %collective-permute-start.1 = (bf16[63,512]{1,0:T(8,128)(2,1)S(1)}, bf16[63,512]{1,0:T(8,128)(2,1)S(1)}, u32[]{:S(2)}, u32[]{:S(2)}) collective-permute-start(bf16[63,512]{1,0:T(8,128)(2,1)S(1)} %slice.32), channel_id=1, source_target_pairs={{0,8},{8,16},{16,24},{24,32},{32,40},{40,48},{48,56},{56,64},{64,7... | collective-permute-start | bytes 193544 | tf_op jit(solution)/shard_map/ppermute | solution.py:14
  513.7 56.6 %copy-start.1 = (bf16[8,2,128,512]{3,2,1,0:T(8,128)(2,1)S(1)}, bf16[8,2,128,512]{3,2,1,0:T(8,128)(2,1)}, u32[]{:S(2)}) copy-start(bf16[8,2,128,512]{3,2,1,0:T(8,128)(2,1)} %param.9) | copy-start | bytes 6291460
Sparse Core Ops, SparseCore 0:
  47.6 182.7 all-gather.2
  232.8 241.5 all-gather.4
  513.9 56.3 reduce-scatter.1
where the time goes:
time: 577 us
  waiting for transfers between devices  484 us (84%)
  local copies, waits for them, and re-layouts  29.8 us (5%)
  blocking collectives  19.9 us (3%)
  matrix products  16.4 us (3%)
  between operations  13.4 us (2%)
  starting transfers between devices  10.2 us (2%)
    all_to_all x1, waiting for transfers between devices, local(): lax.all_to_all(served, 'seq', split_axis=0, concat_axis=0, tiled=True)  202 us
    all_gather x1, waiting for transfers between devices, local(): lax.all_gather(w_query, 'seq', axis=0, tiled=True)  185 us
    reduce_scatter x1, waiting for transfers between devices, local(): lax.psum_scatter(terms.astype(jnp.bfloat16), 'head', scatter_dimension=1,...  56.6 us
    ppermute x2, waiting for transfers between devices, shifted(): return lax.ppermute(shard, axis, pairs)  39.2 us
    all_to_all x1, blocking collectives, local(): lax.all_to_all(slot_table, 'seq', split_axis=0, concat_axis=0, tiled=True)  19.9 us
  transfers between devices with their start and end apart: 6, of which 5 were waited for; matrix products, arithmetic and copies ran while one was open for 5% of the time, Pallas kernels for 0%

commit v1 on v0

--- a/solution.py
+++ b/solution.py
@@ -55,7 +55,9 @@
     next_starts = position == nseq - 1
     queries = jnp.dot(
         states,
-        lax.all_gather(w_query, "seq", axis=0, tiled=True),
+        jnp.concatenate(
+            lax.all_to_all(jnp.stack([w_query] * lax.axis_size("seq")), "seq", 0, 0), axis=0
+        ),
         preferred_element_type=jnp.float32,
     ).astype(jnp.bfloat16)
     leading = shifted(queries[: STRETCH - 1], "seq", -1)

time: 577 us -> 640 us (1.11)
  waiting for transfers between devices: 484 us -> 525 us
  starting transfers between devices: 10.2 us -> 27.9 us
    all_gather x1 -> x0, waiting for transfers between devices: 185 us -> none  [local(): lax.all_gather(w_query, 'seq', axis=0, tiled=True)]
    all_to_all x1, waiting for transfers between devices: 202 us -> 327 us  [local(): lax.all_to_all(served, 'seq', split_axis=0, concat_axis=0, tiled=True)]
    all_to_all x0 -> x1, waiting for transfers between devices: none -> 83.4 us  [local(): lax.all_to_all(jnp.stack([w_query] * lax.axis_size('seq')), 'seq', 0, 0)]
    ppermute x2, waiting for transfers between devices: 39.2 us -> 54.3 us  [shifted(): return lax.ppermute(shard, axis, pairs)]
    ppermute x2, starting transfers between devices: 3.84 us -> 13.5 us  [shifted(): return lax.ppermute(shard, axis, pairs)]
  transfers between devices with their start and end apart: 6 -> 6, of which waited for: 5 -> 5; matrix products, arithmetic and copies ran while one was open for 5% -> 6% of each run, Pallas kernels for 0% -> 0%
where the time goes in v1:
time: 640 us; the launch traced here: 639 us
  waiting for transfers between devices  525 us (82%)
  local copies, waits for them, and re-layouts  33.1 us (5%)
  starting transfers between devices  27.9 us (4%)
  blocking collectives  19.9 us (3%)
  matrix products  16.4 us (3%)
  between operations  13.7 us (2%)
    all_to_all x1, waiting for transfers between devices, local(): lax.all_to_all(served, 'seq', split_axis=0, concat_axis=0, tiled=True)  327 us
    all_to_all x1, waiting for transfers between devices, local(): lax.all_to_all(jnp.stack([w_query] * lax.axis_size('seq')), 'seq', 0, 0)  83.4 us
    reduce_scatter x1, waiting for transfers between devices, local(): lax.psum_scatter(terms.astype(jnp.bfloat16), 'head', scatter_dimension=1,...  59.6 us
    ppermute x2, waiting for transfers between devices, shifted(): return lax.ppermute(shard, axis, pairs)  54.3 us
    all_to_all x1, blocking collectives, local(): lax.all_to_all(slot_table, 'seq', split_axis=0, concat_axis=0, tiled=True)  19.9 us
    ppermute x2, starting transfers between devices, shifted(): return lax.ppermute(shard, axis, pairs)  13.5 us
  transfers between devices with their start and end apart: 6, of which 5 were waited for; matrix products, arithmetic and copies ran while one was open for 6% of the time, Pallas kernels for 0%

profile of v1, /device:TPU:2, one launch (start us, length us, event | category | flops | bytes accessed | tf_op | source)
XLA Modules:
  0.0 639.1 jit_solution(4973494611667229756)
XLA Ops:
  6.5 0.9 copy.26
  7.5 0.9 select_reduce_fusion
  8.4 0.2 convert_reduce_fusion.1
  8.6 0.6 scatter_custom_fusion
  9.3 19.9 %all_to_all.19 = s32[32,1,2]{2,1,0:T(1,128)S(1)} all-to-all(s32[32,1,2]{2,1,0:T(1,128)S(1)} %bitcast.63), channel_id=1, replica_groups=mesh['seq'=32,'head'=8] {'seq'}, dimensions={0} | all-to-all | bytes 512 | tf_op jit(solution)/shard_map/all_to_all | solution.py:86
  29.3 3.4 stack.2
  32.7 5.9 all-to-all-start.2
  38.6 0.5 broadcast.200
  39.1 0.7 reduce.3
  39.9 7.3 %gather_fusion = bf16[64,2,128,512]{3,2,1,0:T(8,128)(2,1)} fusion(bf16[8,2,128,512]{3,2,1,0:T(8,128)(2,1)S(1)} %copy-done, s32[1024]{0:T(1024)S(1)} %pad_clamp_fusion.1), kind=kCustom, calls=%fused_computation | custom fusion | bytes 33554688 | tf_op jit(solution)/shard_map/gather | solution.py:87
  47.2 83.4 %all-to-all-done.2 = bf16[32,128,512]{2,1,0:T(8,128)(2,1)} async-done(((bf16[32,128,512]{2,1,0:T(8,128)(2,1)}), bf16[32,128,512]{2,1,0:T(8,128)(2,1)}, u32[]{:S(2)}, u32[]{:S(2)}) %all-to-all-start.2) | async-done | bytes 4194336 | tf_op jit(solution)/shard_map/all_to_all | solution.py:59
  130.6 8.5 %all-to-all-start.1 = ((bf16[32,2,2,128,512]{4,3,2,1,0:T(8,128)(2,1)}), bf16[32,2,2,128,512]{4,3,2,1,0:T(8,128)(2,1)}, u32[]{:S(2)}, u32[]{:S(2)}) async-start(bf16[32,2,2,128,512]{4,3,2,1,0:T(8,128)(2,1)} %bitcast.55), calls=%async_computation.1 | async-start | bytes 33554432 | tf_op jit(solution)/shard_map/all_to_all | solution.py:88
  139.1 0.7 all-gather.2.cloned.1.call-update
  139.8 5.8 convolution_convert_fusion.1
  145.7 2.2 collective-permute-start
  148.0 48.8 %collective-permute-done = bf16[63,512]{1,0:T(8,128)(2,1)S(1)} collective-permute-done((bf16[63,512]{1,0:T(8,128)(2,1)S(1)}, bf16[63,512]{1,0:T(8,128)(2,1)S(1)}, u32[]{:S(2)}, u32[]{:S(2)}) %collective-permute-start) | collective-permute-done | bytes 64544 | tf_op jit(solution)/shard_map/ppermute | solution.py:14
  197.0 0.3 reshape_reshape.3
  197.3 326.6 %all-to-all-done.1 = bf16[32,2,2,128,512]{4,3,2,1,0:T(8,128)(2,1)} async-done(((bf16[32,2,2,128,512]{4,3,2,1,0:T(8,128)(2,1)}), bf16[32,2,2,128,512]{4,3,2,1,0:T(8,128)(2,1)}, u32[]{:S(2)}, u32[]{:S(2)}) %all-to-all-start.1) | async-done | bytes 16777248 | tf_op jit(solution)/shard_map/all_to_all | solution.py:88
  523.8 8.5 %gather_fusion.1 = bf16[16,2,128,512]{3,2,1,0:T(8,128)(2,1)} fusion(bf16[64,2,128,512]{3,2,1,0:T(8,128)(2,1)} %bitcast.6, s32[1024]{0:T(1024)S(1)} %pad_clamp_fusion), kind=kCustom, calls=%fused_computation.1 | custom fusion | bytes 8388672 | tf_op jit(solution)/shard_map/gather | solution.py:89
  532.3 4.0 fusion.15
  536.3 3.9 copy.29
  540.3 2.4 copy.28
  542.7 2.4 multiply_reduce_fusion.1
  545.1 1.3 convert_reduce_fusion
  546.4 0.2 copy-done.2
  546.6 1.8 multiply_reduce_fusion
  548.4 0.3 divide_convert_fusion
  548.8 0.4 copy.33
  549.3 11.3 %collective-permute-start.1 = (bf16[63,512]{1,0:T(8,128)(2,1)S(1)}, bf16[63,512]{1,0:T(8,128)(2,1)S(1)}, u32[]{:S(2)}, u32[]{:S(2)}) collective-permute-start(bf16[63,512]{1,0:T(8,128)(2,1)S(1)} %slice.32), channel_id=1, source_target_pairs={{0,8},{8,16},{16,24},{24,32},{32,40},{40,48},{48,56},{56,64},{64,7... | collective-permute-start | bytes 193544 | tf_op jit(solution)/shard_map/ppermute | solution.py:14
  560.6 5.5 collective-permute-done.1
  566.1 6.5 %convolution_convert_fusion = bf16[512,4096]{1,0:T(8,128)(2,1)} fusion(bf16[512,4096]{1,0:T(8,128)(2,1)} %all-gather.2.cloned.1.call-done, bf16[449,512]{1,0:T(8,128)(2,1)S(1)} %slice.33, bf16[63,512]{1,0:T(8,128)(2,1)S(1)} %broadcast_select_fusion.1), kind=kOutput, calls=%fused_computation.3 | convolution fusion | flops 2150629376 | bytes 8912896 | tf_op jit(solution)/shard_map/dot_general | solution.py:101
  572.6 59.6 %reduce-scatter.2.cloned.1.call-done = bf16[512,512]{1,0:T(8,128)(2,1)} async-done(((bf16[512,4096]{1,0:T(8,128)(2,1)}), bf16[512,512]{1,0:T(8,128)(2,1)}) %reduce-scatter.2.cloned.1.call-update) | async-done | bytes 524304 | tf_op jit(solution)/shard_map/reduce_scatter | solution.py:106
  (28 shorter events, 0.9 us)
Async XLA Ops:
  6.5 33.4 %copy-start = (bf16[8,2,128,512]{3,2,1,0:T(8,128)(2,1)S(1)}, bf16[8,2,128,512]{3,2,1,0:T(8,128)(2,1)}, u32[]{:S(2)}) copy-start(bf16[8,2,128,512]{3,2,1,0:T(8,128)(2,1)} %param.9) | copy-start | bytes 6291460
  32.7 97.9 %all-to-all-start.2 = ((bf16[32,128,512]{2,1,0:T(8,128)(2,1)}), bf16[32,128,512]{2,1,0:T(8,128)(2,1)}, u32[]{:S(2)}, u32[]{:S(2)}) async-start(bf16[32,128,512]{2,1,0:T(8,128)(2,1)} %stack.2), calls=%async_computation.2 | async-start | bytes 8388608 | tf_op jit(solution)/shard_map/all_to_all | solution.py:59
  130.6 393.3 %all-to-all-start.1 = ((bf16[32,2,2,128,512]{4,3,2,1,0:T(8,128)(2,1)}), bf16[32,2,2,128,512]{4,3,2,1,0:T(8,128)(2,1)}, u32[]{:S(2)}, u32[]{:S(2)}) async-start(bf16[32,2,2,128,512]{4,3,2,1,0:T(8,128)(2,1)} %bitcast.55), calls=%async_computation.1 | async-start | bytes 33554432 | tf_op jit(solution)/shard_map/all_to_all | solution.py:88
  139.1 427.1 %all-gather.2.cloned.1.call-start = ((), (), s32[]{:S(2)}) async-start(), calls=%async_computation.4 | async-start | bytes 4325376 | tf_op jit(solution)/shard_map/all_gather | solution.py:103
  139.8 492.4 %reduce-scatter.2.cloned.1.call-start = ((), (), s32[]{:S(2)}) async-start(), calls=%async_computation.5 | async-start | bytes 4718592 | tf_op jit(solution)/shard_map/reduce_scatter | solution.py:106
  145.7 51.2 %collective-permute-start = (bf16[63,512]{1,0:T(8,128)(2,1)S(1)}, bf16[63,512]{1,0:T(8,128)(2,1)S(1)}, u32[]{:S(2)}, u32[]{:S(2)}) collective-permute-start(bf16[63,512]{1,0:T(8,128)(2,1)S(1)} %slice.30), channel_id=1, source_target_pairs={{8,0},{16,8},{24,16},{32,24},{40,32},{48,40},{56,48},{64,56},{72,6... | collective-permute-start | bytes 193544 | tf_op jit(solution)/shard_map/ppermute | solution.py:14
  545.0 1.6 copy-start.2
  549.3 16.8 %collective-permute-start.1 = (bf16[63,512]{1,0:T(8,128)(2,1)S(1)}, bf16[63,512]{1,0:T(8,128)(2,1)S(1)}, u32[]{:S(2)}, u32[]{:S(2)}) collective-permute-start(bf16[63,512]{1,0:T(8,128)(2,1)S(1)} %slice.32), channel_id=1, source_target_pairs={{0,8},{8,16},{16,24},{24,32},{32,40},{40,48},{48,56},{56,64},{64,7... | collective-permute-start | bytes 193544 | tf_op jit(solution)/shard_map/ppermute | solution.py:14
  572.6 59.6 %copy-start.1 = (bf16[8,2,128,512]{3,2,1,0:T(8,128)(2,1)S(1)}, bf16[8,2,128,512]{3,2,1,0:T(8,128)(2,1)}, u32[]{:S(2)}) copy-start(bf16[8,2,128,512]{3,2,1,0:T(8,128)(2,1)} %param.9) | copy-start | bytes 6291460
Sparse Core Ops, SparseCore 0:
  142.4 227.4 all-gather.1
  572.7 59.4 reduce-scatter.1
